TPU v7x, 32 devices: a whole 2x2x4 slice. The times are simulated.
32 devices in a mesh: row: 4 (over y, x), col: 8 (over z, core).
Axes of the slice: x: 2, y: 2, z: 4, core: 2. Of those that a mesh axis runs over, the one named last changes fastest.
Arguments:
- query_states: bfloat16 [4, 8, 128, 768], P('row', 'col'), may hold values from -15 to 15
- key_states: bfloat16 [4, 8, 128, 768], P('row', 'col'), may hold values from -6 to 6
- value_states: bfloat16 [4, 8, 128, 768], P('row', 'col'), may hold values from -6 to 6
- tissue_map: int32 [4, 8], replicated, may hold values 0 or 1
Outputs:
- attended: bfloat16 [4, 8, 128, 768], P('row', 'col')
All inputs are finite; a program needn't handle non-finite values.
Results may differ from a plain program's by a relative error of at most 0.0032.
Values may be sent and summed in bfloat16 or wider, within the bound.
A program may use at most 64 MiB of HBM per device.

v0:
```python
import jax
import jax.numpy as jnp
from jax import lax
from jax.sharding import PartitionSpec as P

HDIM = 64
HEADS = 12


def extended(x, sides, width):
    for axis, dim in sides:
        devices, length = (lax.axis_size(axis), x.shape[dim])
        up = [(i, (i + 1) % devices) for i in range(devices - 1)]
        down = [(j, i) for i, j in up]
        last = lax.slice_in_dim(x, length - width, length, axis=dim)
        initial = lax.slice_in_dim(x, 0, width, axis=dim)
        before = lax.ppermute(last, axis, up)
        after = lax.ppermute(initial, axis, down)
        x = jnp.concatenate([before, x, after], axis=dim)
    return x


def attend_row(query_row, keys_row, values_row, key_keep, own_tile):
    score_scale = HDIM ** (-0.5)
    tile_count = query_row.shape[0]
    tokens = query_row.shape[1]
    query_heads = query_row.reshape(tile_count, tokens, HEADS, HDIM)
    key_heads = keys_row.reshape(tile_count, keys_row.shape[1], HEADS, HDIM)
    value_heads = values_row.reshape(tile_count, values_row.shape[1], HEADS, HDIM)
    scores = (
        jnp.einsum("bqhd,bkhd->bhqk", query_heads, key_heads, preferred_element_type=jnp.float32)
        * score_scale
    )
    scores = jnp.where(key_keep[:, None, None, :], scores, -jnp.inf)
    row_top = jnp.max(scores, axis=-1, keepdims=True)
    weights = jnp.exp(scores - row_top)
    totals = jnp.sum(weights, axis=-1)
    rounded = weights.astype(jnp.bfloat16)
    mixed = jnp.einsum("bhqk,bkhd->bqhd", rounded, value_heads, preferred_element_type=jnp.float32)
    mixed = mixed / jnp.transpose(totals, (0, 2, 1))[:, :, :, None]
    mixed = mixed * own_tile[:, None, None, None]
    return mixed.reshape(tile_count, tokens, HEADS * HDIM).astype(jnp.bfloat16)


def on_device(query_states, key_states, value_states, tissue_map):
    tile_rows = query_states.shape[0]
    tile_cols = query_states.shape[1]
    tokens = query_states.shape[2]
    paired = jnp.stack([key_states, value_states])
    padded = extended(paired, (("row", 1), ("col", 2)), 1)
    row_start = lax.axis_index("row") * tile_rows
    col_start = lax.axis_index("col") * tile_cols
    framed = jnp.pad(tissue_map, 1)
    nearby = lax.dynamic_slice(framed, (row_start, col_start), (tile_rows + 2, tile_cols + 2))
    centre = jnp.arange(9) == 4
    pieces = []
    markers = []
    for row_off in range(3):
        for col_off in range(3):
            pieces.append(padded[:, row_off, col_off : col_off + tile_cols])
            markers.append(nearby[row_off, col_off : col_off + tile_cols])
    gathered = jnp.concatenate(pieces, axis=2)
    present = (jnp.stack(markers, axis=1) > 0) | centre[None, :]
    key_keep = jnp.repeat(present, tokens, axis=1)
    own_tile = nearby[1, 1 : 1 + tile_cols].astype(jnp.float32)
    results = [attend_row(query_states[0], gathered[0], gathered[1], key_keep, own_tile)]
    return jnp.stack(results)


def solution(mesh):
    return jax.shard_map(
        on_device,
        mesh=mesh,
        in_specs=(
            P("row", "col", None, None),
            P("row", "col", None, None),
            P("row", "col", None, None),
            P(),
        ),
        out_specs=P("row", "col", None, None),
        check_vma=False,
    )
```

profile of v0, /device:TPU:5, one launch (start us, length us, event | category | flops | bytes accessed | tf_op | source)
XLA Modules:
  0.0 57.2 jit_solution(16941019680261854289)
XLA Ops:
  0.0 0.0 copy-start.2
  0.0 0.0 copy-start.3
  0.0 1.1 %fusion.24 = bf16[2,1,1,128,768]{4,3,0,2,1:T(8,128)(2,1)S(1)} fusion(bf16[1,1,1,128,768]{4,3,2,1,0:T(8,128)(2,1)} %bitcast.87, bf16[1,1,1,128,768]{4,3,2,1,0:T(8,128)(2,1)} %bitcast.89), kind=kLoop, calls=%fused_computation.29 | loop fusion | flops 196608 | bytes 786432 | tf_op jit(solution)/shard_map/stack | solution.py:49
  1.1 3.1 %collective-permute-start.1 = (bf16[2,1,1,128,768]{4,3,0,2,1:T(8,128)(2,1)S(1)}, bf16[2,1,1,128,768]{4,3,0,2,1:T(8,128)(2,1)S(1)}, u32[]{:S(2)}, u32[]{:S(2)}) collective-permute-start(bf16[2,1,1,128,768]{4,3,0,2,1:T(8,128)(2,1)S(1)} %fusion.24), channel_id=1, source_target_pairs={{8,0},{16,8},{24,16},{9,1},{17,9},{25,17},{10,2},{18,10},{26,18},{... | collective-permute-start | bytes 1179656 | tf_op jit(solution)/shard_map/ppermute | solution.py:18
  4.2 2.2 %collective-permute-start = (bf16[2,1,1,128,768]{4,3,0,2,1:T(8,128)(2,1)S(1)}, bf16[2,1,1,128,768]{4,3,0,2,1:T(8,128)(2,1)S(1)}, u32[]{:S(2)}, u32[]{:S(2)}) collective-permute-start(bf16[2,1,1,128,768]{4,3,0,2,1:T(8,128)(2,1)S(1)} %fusion.24), channel_id=1, source_target_pairs={{0,8},{8,16},{16,24},{1,9},{9,17},{17,25},{2,10},{10,18},{18,26},{... | collective-permute-start | bytes 1179656 | tf_op jit(solution)/shard_map/ppermute | solution.py:17
  6.4 6.6 %collective-permute-done.1 = bf16[2,1,1,128,768]{4,3,0,2,1:T(8,128)(2,1)S(1)} collective-permute-done((bf16[2,1,1,128,768]{4,3,0,2,1:T(8,128)(2,1)S(1)}, bf16[2,1,1,128,768]{4,3,0,2,1:T(8,128)(2,1)S(1)}, u32[]{:S(2)}, u32[]{:S(2)}) %collective-permute-start.1) | collective-permute-done | bytes 393248 | tf_op jit(solution)/shard_map/ppermute | solution.py:18
  13.0 8.4 %collective-permute-done = bf16[2,1,1,128,768]{4,3,0,2,1:T(8,128)(2,1)S(1)} collective-permute-done((bf16[2,1,1,128,768]{4,3,0,2,1:T(8,128)(2,1)S(1)}, bf16[2,1,1,128,768]{4,3,0,2,1:T(8,128)(2,1)S(1)}, u32[]{:S(2)}, u32[]{:S(2)}) %collective-permute-start) | collective-permute-done | bytes 393248 | tf_op jit(solution)/shard_map/ppermute | solution.py:17
  21.4 1.1 %pad_maximum_fusion = bf16[2,3,1,128,768]{4,3,0,2,1:T(8,128)(2,1)} fusion(bf16[2,1,1,128,768]{4,3,0,2,1:T(8,128)(2,1)S(1)} %collective-permute-done.1, bf16[2,1,1,128,768]{4,3,0,2,1:T(8,128)(2,1)S(1)} %fusion.24, bf16[2,1,1,128,768]{4,3,0,2,1:T(8,128)(2,1)S(1)} %collective-permute-done), kind=kLoop, calls=%fused_computation.9 | loop fusion | flops 1179648 | bytes 2359296 | tf_op jit(solution)/shard_map/concatenate | solution.py:19
  22.6 4.5 %collective-permute-start.2 = (bf16[2,3,1,128,768]{4,3,0,2,1:T(8,128)(2,1)}, bf16[2,3,1,128,768]{4,3,0,2,1:T(8,128)(2,1)S(1)}, u32[]{:S(2)}, u32[]{:S(2)}) collective-permute-start(bf16[2,3,1,128,768]{4,3,0,2,1:T(8,128)(2,1)} %pad_maximum_fusion), channel_id=1, source_target_pairs={{0,1},{1,2},{2,3},{3,4},{4,5},{5,6},{6,7},{8,9},{9,10},{10,11},{11... | collective-permute-start | bytes 3538952 | tf_op jit(solution)/shard_map/ppermute | solution.py:17
  27.1 1.9 %collective-permute-start.3 = (bf16[2,3,1,128,768]{4,3,0,2,1:T(8,128)(2,1)}, bf16[2,3,1,128,768]{4,3,0,2,1:T(8,128)(2,1)S(1)}, u32[]{:S(2)}, u32[]{:S(2)}) collective-permute-start(bf16[2,3,1,128,768]{4,3,0,2,1:T(8,128)(2,1)} %pad_maximum_fusion), channel_id=1, source_target_pairs={{1,0},{2,1},{3,2},{4,3},{5,4},{6,5},{7,6},{9,8},{10,9},{11,10},{12... | collective-permute-start | bytes 3538952 | tf_op jit(solution)/shard_map/ppermute | solution.py:18
  29.1 0.8 %pad_dynamic-slice_fusion = s32[3,3]{1,0:T(4,128)S(1)} fusion(s32[]{:T(128)S(6)} %select_n.14, s32[]{:T(128)S(6)} %select_n.15, s32[4,8]{1,0:T(4,128)} %param.7), kind=kLoop, calls=%fused_computation.30 | loop fusion | bytes 172 | tf_op jit(solution)/shard_map/dynamic_slice | solution.py:54
  29.8 0.6 %slice.56 = s32[1,1]{1,0:T(1,128)} slice(s32[3,3]{1,0:T(4,128)S(1)} %pad_dynamic-slice_fusion), slice={[1:2], [1:2]} | slice | bytes 8 | tf_op jit(solution)/shard_map/slice | solution.py:61
  31.1 1.7 %copy.18 = bf16[1,1,128,768]{2,3,1,0:T(8,128)(2,1)} copy(bf16[1,1,128,768]{3,2,1,0:T(8,128)(2,1)} %param.4) | data formatting | bytes 393216 | tf_op args[0]
  32.8 0.1 compare_or_fusion
  32.9 0.1 broadcast_bitcast_fusion
  33.0 7.6 %collective-permute-done.2 = bf16[2,3,1,128,768]{4,3,0,2,1:T(8,128)(2,1)S(1)} collective-permute-done((bf16[2,3,1,128,768]{4,3,0,2,1:T(8,128)(2,1)}, bf16[2,3,1,128,768]{4,3,0,2,1:T(8,128)(2,1)S(1)}, u32[]{:S(2)}, u32[]{:S(2)}) %collective-permute-start.2) | collective-permute-done | bytes 1179680 | tf_op jit(solution)/shard_map/ppermute | solution.py:17
  40.6 4.2 %collective-permute-done.3 = bf16[2,3,1,128,768]{4,3,0,2,1:T(8,128)(2,1)S(1)} collective-permute-done((bf16[2,3,1,128,768]{4,3,0,2,1:T(8,128)(2,1)}, bf16[2,3,1,128,768]{4,3,0,2,1:T(8,128)(2,1)S(1)}, u32[]{:S(2)}, u32[]{:S(2)}) %collective-permute-start.3) | collective-permute-done | bytes 1179680 | tf_op jit(solution)/shard_map/ppermute | solution.py:18
  44.9 0.0 copy-done.2
  44.9 0.0 copy-done.3
  45.1 0.2 fusion.27
  45.4 2.2 %copy.17 = bf16[1,1,1152,768]{2,3,1,0:T(8,128)(2,1)} copy(bf16[1,1,1152,768]{3,2,0,1:T(8,128)(2,1)S(1)} %get-tuple-element.5) | data formatting | bytes 3538944 | tf_op jit(solution)/shard_map/slice | solution.py:66
  47.6 0.0 copy-start
  47.6 2.2 %copy.16 = bf16[1,1,1152,768]{2,3,1,0:T(8,128)(2,1)} copy(bf16[1,1,1152,768]{3,2,0,1:T(8,128)(2,1)S(1)} %get-tuple-element.6) | data formatting | bytes 3538944 | tf_op jit(solution)/shard_map/slice | solution.py:66
  49.9 0.0 copy-done
  49.9 2.6 %bitcast_reduce_fusion = (f32[12,128]{1,0:T(8,128)S(1)}, f32[12,1152,128]{2,1,0:T(8,128)S(1)}) fusion(pred[1152]{0:T(1024)(128)(4,1)S(1)} %broadcast_bitcast_fusion, bf16[1152,12,64]{0,2,1:T(8,128)(2,1)S(1)} %bitcast.85, bf16[128,12,64]{0,2,1:T(8,128)(2,1)} %bitcast.91), kind=kOutput, calls=%fused_computation.1 | convolution fusion | flops 231799296 | bytes 9051264 | tf_op jit(solution)/shard_map/bqhd,bkhd->bhqk/dot_general | solution.py:31
  52.5 0.0 copy-start.1
  52.5 1.9 %fusion.1 = f32[12,128]{1,0:T(8,128)S(1)} fusion(f32[12,1152,128]{2,1,0:T(8,128)S(1)} %get-tuple-element.11, f32[12,128]{1,0:T(8,128)S(1)} %get-tuple-element.10, pred[1152]{0:T(1024)(128)(4,1)S(1)} %broadcast_bitcast_fusion), kind=kLoop, calls=%fused_computation.4 | loop fusion | flops 7076352 | bytes 7091328 | tf_op jit(solution)/shard_map/reduce_sum | solution.py:37
  54.4 0.0 copy-done.1
  54.4 1.9 %fusion.15 = bf16[1,128,12,64]{1,3,2,0:T(8,128)(2,1)S(1)} fusion(bf16[1152,12,64]{0,2,1:T(8,128)(2,1)S(1)} %bitcast.86, f32[12,1152,128]{2,1,0:T(8,128)S(1)} %get-tuple-element.11, f32[12,128]{1,0:T(8,128)S(1)} %get-tuple-element.10, pred[1152]{0:T(1024)(128)(4,1)S(1)} %broadcast_bitcast_fusion, f32[]{:T(128)} %bitcast.27, f32[128,12]{0,1:T(8,128)S(1)} %bitcast.93), kind=kOutput, calls=%fused_computation.12 | convolution fusion | flops 233865216 | bytes 9057412 | tf_op jit(solution)/shard_map/bhqk,bkhd->bqhd/dot_general | solution.py:39
  56.3 0.8 %copy.20 = bf16[1,1,128,768]{3,2,1,0:T(8,128)(2,1)} copy(bf16[1,1,128,768]{2,3,1,0:T(8,128)(2,1)S(1)} %bitcast.92) | data formatting | bytes 393216 | tf_op jit(solution)/shard_map/convert_element_type | solution.py:42
  (10 shorter events, 0.3 us)
Async XLA Ops:
  0.0 44.9 %copy-start.2 = (bf16[1,1,128,768]{3,2,1,0:T(8,128)(2,1)S(1)}, bf16[1,1,128,768]{3,2,1,0:T(8,128)(2,1)}, u32[]{:S(2)}) copy-start(bf16[1,1,128,768]{3,2,1,0:T(8,128)(2,1)} %param.6) | copy-start | bytes 589828
  0.0 44.9 %copy-start.3 = (bf16[1,1,128,768]{3,2,1,0:T(8,128)(2,1)S(1)}, bf16[1,1,128,768]{3,2,1,0:T(8,128)(2,1)}, u32[]{:S(2)}) copy-start(bf16[1,1,128,768]{3,2,1,0:T(8,128)(2,1)} %param.5) | copy-start | bytes 589828
  1.1 11.9 %collective-permute-start.1 = (bf16[2,1,1,128,768]{4,3,0,2,1:T(8,128)(2,1)S(1)}, bf16[2,1,1,128,768]{4,3,0,2,1:T(8,128)(2,1)S(1)}, u32[]{:S(2)}, u32[]{:S(2)}) collective-permute-start(bf16[2,1,1,128,768]{4,3,0,2,1:T(8,128)(2,1)S(1)} %fusion.24), channel_id=1, source_target_pairs={{8,0},{16,8},{24,16},{9,1},{17,9},{25,17},{10,2},{18,10},{26,18},{... | collective-permute-start | bytes 1179656 | tf_op jit(solution)/shard_map/ppermute | solution.py:18
  4.2 17.3 %collective-permute-start = (bf16[2,1,1,128,768]{4,3,0,2,1:T(8,128)(2,1)S(1)}, bf16[2,1,1,128,768]{4,3,0,2,1:T(8,128)(2,1)S(1)}, u32[]{:S(2)}, u32[]{:S(2)}) collective-permute-start(bf16[2,1,1,128,768]{4,3,0,2,1:T(8,128)(2,1)S(1)} %fusion.24), channel_id=1, source_target_pairs={{0,8},{8,16},{16,24},{1,9},{9,17},{17,25},{2,10},{10,18},{18,26},{... | collective-permute-start | bytes 1179656 | tf_op jit(solution)/shard_map/ppermute | solution.py:17
  22.6 18.0 %collective-permute-start.2 = (bf16[2,3,1,128,768]{4,3,0,2,1:T(8,128)(2,1)}, bf16[2,3,1,128,768]{4,3,0,2,1:T(8,128)(2,1)S(1)}, u32[]{:S(2)}, u32[]{:S(2)}) collective-permute-start(bf16[2,3,1,128,768]{4,3,0,2,1:T(8,128)(2,1)} %pad_maximum_fusion), channel_id=1, source_target_pairs={{0,1},{1,2},{2,3},{3,4},{4,5},{5,6},{6,7},{8,9},{9,10},{10,11},{11... | collective-permute-start | bytes 3538952 | tf_op jit(solution)/shard_map/ppermute | solution.py:17
  27.1 17.7 %collective-permute-start.3 = (bf16[2,3,1,128,768]{4,3,0,2,1:T(8,128)(2,1)}, bf16[2,3,1,128,768]{4,3,0,2,1:T(8,128)(2,1)S(1)}, u32[]{:S(2)}, u32[]{:S(2)}) collective-permute-start(bf16[2,3,1,128,768]{4,3,0,2,1:T(8,128)(2,1)} %pad_maximum_fusion), channel_id=1, source_target_pairs={{1,0},{2,1},{3,2},{4,3},{5,4},{6,5},{7,6},{9,8},{10,9},{11,10},{12... | collective-permute-start | bytes 3538952 | tf_op jit(solution)/shard_map/ppermute | solution.py:18
  47.6 2.2 %copy-start = (bf16[1,1,1152,768]{2,3,1,0:T(8,128)(2,1)S(1)}, bf16[1,1,1152,768]{2,3,1,0:T(8,128)(2,1)}, u32[]{:S(2)}) copy-start(bf16[1,1,1152,768]{2,3,1,0:T(8,128)(2,1)} %copy.17) | copy-start | bytes 5308420
  52.5 1.9 %copy-start.1 = (bf16[1,1,1152,768]{2,3,1,0:T(8,128)(2,1)S(1)}, bf16[1,1,1152,768]{2,3,1,0:T(8,128)(2,1)}, u32[]{:S(2)}) copy-start(bf16[1,1,1152,768]{2,3,1,0:T(8,128)(2,1)} %copy.16) | copy-start | bytes 5308420
where the time goes:
time: 57.4 us; the launch traced here: 57.2 us
  waiting for transfers between devices  26.8 us (47%)
  starting transfers between devices  11.8 us (21%)
  local copies, waits for them, and re-layouts  8.95 us (16%)
  matrix products  4.51 us (8%)
  other arithmetic  4.28 us (7%)
  between operations  0.82 us (1%)
    ppermute x2, waiting for transfers between devices, extended(): before = lax.ppermute(last, axis, up)  16 us
    ppermute x2, waiting for transfers between devices, extended(): after = lax.ppermute(initial, axis, down)  10.8 us
    ppermute x2, starting transfers between devices, extended(): before = lax.ppermute(last, axis, up)  6.79 us
    ppermute x2, starting transfers between devices, extended(): after = lax.ppermute(initial, axis, down)  4.98 us
    dot_general x1, matrix products, attend_row(): jnp.einsum('bqhd,bkhd->bhqk', query_heads, key_heads, preferred_element_t...  2.61 us
    slice x2, local copies, waits for them, and re-layouts, on_device(): gathered[0]  2.47 us
    slice x1, local copies, waits for them, and re-layouts, on_device(): gathered[1]  2.24 us
    unnamed x16, local copies, waits for them, and re-layouts  1.95 us
  transfers between devices with their start and end apart: 4, of which 4 were waited for; matrix products, arithmetic and copies ran while one was open for 6% of the time, Pallas kernels for 0%

commit v1 on v0

v1 whole, which is shorter than its diff:
```python
import functools

import jax
import jax.numpy as jnp
from jax import lax
from jax.experimental import pallas as pl
from jax.experimental.pallas import tpu as pltpu
from jax.sharding import PartitionSpec as P

HDIM = 64
LANES = 128
MESH = pl.DeviceIdType.MESH
LAG = 3


def kernel(rows, cols, tissue, q_hbm, k_hbm, v_hbm, out_ref, kv, qv, bias, local_sem,
           row_send, row_recv, col_send, col_recv):
    chunks, _, _, tokens, _ = kv.shape
    r, c = lax.axis_index("row"), lax.axis_index("col")
    ring = rows == 4
    has_up, has_down = r > 0, r < rows - 1
    has_left, has_right = c > 0, c < cols - 1
    slot = lambda a, b: (a + 1) * 3 + b + 1
    part = lambda i, s: kv.at[i, :, s]

    def lanes(i):
        return pl.ds(pl.multiple_of(i * LANES, LANES), LANES)

    def local_copies(i):
        return [
            pltpu.make_async_copy(k_hbm.at[0, 0, :, lanes(i)], kv.at[i, 0, 4], local_sem.at[0, i]),
            pltpu.make_async_copy(v_hbm.at[0, 0, :, lanes(i)], kv.at[i, 1, 4], local_sem.at[1, i]),
            pltpu.make_async_copy(q_hbm.at[0, 0, :, lanes(i)], qv.at[i], local_sem.at[2, i]),
        ]

    @pl.loop(0, chunks)
    def _(i):
        for copy in local_copies(i):
            copy.start()

    if ring:
        near = 1 - 2 * lax.rem(r, 2)
        outer = jnp.logical_or(r == 0, r == 3)
        inner = jnp.logical_and(r > 0, r < 3)
        across = jnp.where(r < 2, r + 2, r - 2)
        channels = [
            (None, near, None, r + near, slot(0, 0), slot(-near, 0)),
            (inner, -near, outer, across, slot(near, 0), slot(-near, 0)),
        ]
        greet = [(None, r + near), (None, across)]
    else:
        channels = [
            (has_up, -1, has_down, r + 1, slot(0, 0), slot(-1, 0)),
            (has_down, 1, has_up, r - 1, slot(0, 0), slot(1, 0)),
        ]
        greet = [(has_up, r - 1), (has_down, r + 1)]

    def when(cond, f):
        if cond is None:
            f()
        else:
            pl.when(cond)(f)

    barrier = pltpu.get_barrier_semaphore()
    count = 0
    for cond, other in greet:
        when(cond, lambda other=other: pl.semaphore_signal(
            barrier, inc=1, device_id=(other, c), device_id_type=MESH))
        count = count + (1 if cond is None else cond.astype(jnp.int32))
    for cond, other in ((has_left, c - 1), (has_right, c + 1)):
        when(cond, lambda other=other: pl.semaphore_signal(
            barrier, inc=1, device_id=(r, other), device_id_type=MESH))
        count = count + cond.astype(jnp.int32)

    for a in (-1, 0, 1):
        for b in (-1, 0, 1):
            s = slot(a, b)
            if (a, b) == (0, 0):
                bias[:, s * tokens:(s + 1) * tokens] = jnp.zeros((8, tokens), jnp.float32)
                continue
            inside = jnp.logical_and(jnp.logical_and(r + a >= 0, r + a < rows),
                                     jnp.logical_and(c + b >= 0, c + b < cols))
            entry = tissue[jnp.clip(r + a, 0, rows - 1), jnp.clip(c + b, 0, cols - 1)]
            live = jnp.where(inside, entry, 0) > 0
            shift = jnp.where(live, jnp.float32(0), jnp.float32(-jnp.inf))
            bias[:, s * tokens:(s + 1) * tokens] = jnp.full((8, tokens), shift, jnp.float32)

            @pl.when(jnp.logical_not(inside))
            def _():
                @pl.loop(0, chunks)
                def _(i):
                    kv[i, :, s] = jnp.zeros((2, tokens, LANES), kv.dtype)

    pl.semaphore_wait(barrier, count)

    def row_copy(ch, i):
        _, _, _, target, source, landing = channels[ch]
        return pltpu.make_async_remote_copy(
            src_ref=part(i, source), dst_ref=part(i, landing),
            send_sem=row_send.at[ch, i], recv_sem=row_recv.at[ch, i],
            device_id=(target, c), device_id_type=MESH)

    def col_copy(direction, which, i):
        a = 0 if which == 0 else channels[which - 1][1]
        b = -1 if direction == 0 else 1
        return pltpu.make_async_remote_copy(
            src_ref=part(i, slot(a, 0)), dst_ref=part(i, slot(a, b)),
            send_sem=col_send.at[direction, which, i], recv_sem=col_recv.at[direction, which, i],
            device_id=(r, c - b), device_id_type=MESH)

    def col_sends(which, i):
        when(has_right, lambda: col_copy(0, which, i).start())
        when(has_left, lambda: col_copy(1, which, i).start())

    @pl.loop(0, chunks)
    def _(i):
        for copy in local_copies(i):
            copy.wait()
        for ch in (0, 1):
            if not (ring and ch == 1):
                when(channels[ch][2], lambda: row_copy(ch, i).start())
        col_sends(0, i)

    def forward(i):
        for ch in (0, 1):
            def step():
                row_copy(ch, i).wait_recv()
                if ring and ch == 0:
                    when(channels[1][2], lambda: row_copy(1, i).start())
                col_sends(1 + ch, i)
            when(channels[ch][0], step)

    own = tissue[r, c].astype(jnp.float32)
    low = lax.broadcasted_iota(jnp.int32, (tokens, LANES), 1) < HDIM

    def compute(i):
        for direction, cond in ((0, has_left), (1, has_right)):
            for which in (0, 1, 2):
                there = cond
                if which and channels[which - 1][0] is not None:
                    there = jnp.logical_and(cond, channels[which - 1][0])
                when(there, lambda: col_copy(direction, which, i).wait_recv())
        q = qv[i] * jnp.bfloat16(HDIM ** -0.5)
        zero = jnp.zeros_like(q)
        pair = jnp.concatenate([jnp.where(low, q, zero), jnp.where(low, zero, q)], axis=0)
        keys = kv[i, 0].reshape(9 * tokens, LANES)
        values = kv[i, 1].reshape(9 * tokens, LANES)
        scores = lax.dot_general(pair, keys, (((1,), (1,)), ((), ())), preferred_element_type=jnp.float32)
        scores = scores + bias[0:1, :]
        weights = jnp.exp(scores - jnp.max(scores, axis=1, keepdims=True))
        totals = jnp.sum(weights, axis=1, keepdims=True)
        mixed = jnp.dot(weights.astype(jnp.bfloat16), values, preferred_element_type=jnp.float32)
        mixed = mixed / totals * own
        out_ref[0, 0, :, lanes(i)] = jnp.where(low, mixed[:tokens], mixed[tokens:]).astype(out_ref.dtype)

    @pl.loop(0, LAG)
    def _(i):
        forward(i)

    @pl.loop(LAG, chunks)
    def _(i):
        forward(i)
        compute(i - LAG)

    @pl.loop(chunks - LAG, chunks)
    def _(i):
        compute(i)

    @pl.loop(0, chunks)
    def _(i):
        for ch in (0, 1):
            when(channels[ch][2], lambda: row_copy(ch, i).wait_send())
        for which in (0, 1, 2):
            for direction, cond in ((0, has_right), (1, has_left)):
                there = cond
                if which and channels[which - 1][0] is not None:
                    there = jnp.logical_and(cond, channels[which - 1][0])
                when(there, lambda: col_copy(direction, which, i).wait_send())


def on_device(rows, cols, query_states, key_states, value_states, tissue_map):
    _, _, tokens, features = query_states.shape
    chunks = features // LANES
    any_space = pl.BlockSpec(memory_space=pl.ANY)
    return pl.pallas_call(
        functools.partial(kernel, rows, cols),
        out_shape=jax.ShapeDtypeStruct(query_states.shape, jnp.bfloat16),
        in_specs=[pl.BlockSpec(memory_space=pltpu.SMEM), any_space, any_space, any_space],
        out_specs=pl.BlockSpec(memory_space=pltpu.VMEM),
        scratch_shapes=[
            pltpu.VMEM((chunks, 2, 9, tokens, LANES), jnp.bfloat16),
            pltpu.VMEM((chunks, tokens, LANES), jnp.bfloat16),
            pltpu.VMEM((8, 9 * tokens), jnp.float32),
            pltpu.SemaphoreType.DMA((3, chunks)),
            pltpu.SemaphoreType.DMA((2, chunks)),
            pltpu.SemaphoreType.DMA((2, chunks)),
            pltpu.SemaphoreType.DMA((2, 3, chunks)),
            pltpu.SemaphoreType.DMA((2, 3, chunks)),
        ],
        compiler_params=pltpu.CompilerParams(
            collective_id=0, has_side_effects=True, vmem_limit_bytes=40 * 1024 * 1024),
        cost_estimate=pl.CostEstimate(
            flops=4 * 9 * tokens * tokens * features, bytes_accessed=8 * tokens * features,
            transcendentals=9 * tokens * tokens * features // HDIM),
        name="neighbourhood",
    )(tissue_map, query_states, key_states, value_states)


def solution(mesh):
    return jax.shard_map(
        functools.partial(on_device, mesh.shape["row"], mesh.shape["col"]),
        mesh=mesh,
        in_specs=(
            P("row", "col", None, None),
            P("row", "col", None, None),
            P("row", "col", None, None),
            P(),
        ),
        out_specs=P("row", "col", None, None),
        check_vma=False,
    )
```

time: 57.4 us -> 27.4 us (0.48)
  the two profiles are of different devices: /device:TPU:5 before, /device:TPU:3 now
where the time goes in v1:
time: 27.4 us; the launch traced here: 27.2 us
  Pallas kernels  23 us (84%)
  local copies, waits for them, and re-layouts  4.14 us (15%)
    pallas_call x1, Pallas kernels, on_device(): pl.pallas_call(functools.partial(kernel, rows, cols), out_shape=jax.Shape...  23 us
    unnamed x9, local copies, waits for them, and re-layouts  4.14 us

profile of v1, /device:TPU:3, one launch (start us, length us, event | category | flops | bytes accessed | tf_op | source)
XLA Modules:
  0.0 27.2 jit_solution(831445956577581337)
XLA Ops:
  0.0 0.0 copy-start
  0.0 0.9 %copy-done = bf16[1,1,128,768]{3,2,1,0:T(8,128)(2,1)S(1)} copy-done((bf16[1,1,128,768]{3,2,1,0:T(8,128)(2,1)S(1)}, bf16[1,1,128,768]{3,2,1,0:T(8,128)(2,1)}, u32[]{:S(2)}) %copy-start) | copy-done | bytes 196632
  0.9 0.0 copy-start.1
  0.9 0.9 %copy-done.1 = bf16[1,1,128,768]{3,2,1,0:T(8,128)(2,1)S(1)} copy-done((bf16[1,1,128,768]{3,2,1,0:T(8,128)(2,1)S(1)}, bf16[1,1,128,768]{3,2,1,0:T(8,128)(2,1)}, u32[]{:S(2)}) %copy-start.1) | copy-done | bytes 196632
  1.9 0.0 copy-start.2
  1.9 0.9 %copy-done.2 = bf16[1,1,128,768]{3,2,1,0:T(8,128)(2,1)S(1)} copy-done((bf16[1,1,128,768]{3,2,1,0:T(8,128)(2,1)S(1)}, bf16[1,1,128,768]{3,2,1,0:T(8,128)(2,1)}, u32[]{:S(2)}) %copy-start.2) | copy-done | bytes 196632
  2.8 0.0 copy-start.3
  2.8 0.7 %copy-done.3 = s32[4,8]{1,0:T(4,128)S(1)} copy-done((s32[4,8]{1,0:T(4,128)S(1)}, s32[4,8]{1,0:T(4,128)}, u32[]{:S(2)}) %copy-start.3) | copy-done | bytes 152
  3.5 23.0 %neighbourhood.1 = bf16[1,1,128,768]{3,2,1,0:T(8,128)(2,1)S(1)} custom-call(s32[4,8]{1,0:T(4,128)S(1)} %copy-done.3, bf16[1,1,128,768]{3,2,1,0:T(8,128)(2,1)S(1)} %copy-done, bf16[1,1,128,768]{3,2,1,0:T(8,128)(2,1)S(1)} %copy-done.1, bf16[1,1,128,768]{3,2,1,0:T(8,128)(2,1)S(1)} %copy-done.2), custom_call_target="tpu_custom_call" | custom-call | flops 452984832 | bytes 786432 | tf_op jit(solution)/shard_map/neighbourhood/pallas_call | solution.py:185
  26.5 0.7 %copy.6 = bf16[1,1,128,768]{3,2,1,0:T(8,128)(2,1)} copy(bf16[1,1,128,768]{3,2,1,0:T(8,128)(2,1)S(1)} %neighbourhood.1) | data formatting | bytes 393216
Async XLA Ops:
  0.0 0.9 %copy-start = (bf16[1,1,128,768]{3,2,1,0:T(8,128)(2,1)S(1)}, bf16[1,1,128,768]{3,2,1,0:T(8,128)(2,1)}, u32[]{:S(2)}) copy-start(bf16[1,1,128,768]{3,2,1,0:T(8,128)(2,1)} %q_hbm.1) | copy-start | bytes 589828
  0.9 0.9 %copy-start.1 = (bf16[1,1,128,768]{3,2,1,0:T(8,128)(2,1)S(1)}, bf16[1,1,128,768]{3,2,1,0:T(8,128)(2,1)}, u32[]{:S(2)}) copy-start(bf16[1,1,128,768]{3,2,1,0:T(8,128)(2,1)} %k_hbm.1) | copy-start | bytes 589828
  1.9 0.9 %copy-start.2 = (bf16[1,1,128,768]{3,2,1,0:T(8,128)(2,1)S(1)}, bf16[1,1,128,768]{3,2,1,0:T(8,128)(2,1)}, u32[]{:S(2)}) copy-start(bf16[1,1,128,768]{3,2,1,0:T(8,128)(2,1)} %v_hbm.1) | copy-start | bytes 589828
  2.8 0.7 %copy-start.3 = (s32[4,8]{1,0:T(4,128)S(1)}, s32[4,8]{1,0:T(4,128)}, u32[]{:S(2)}) copy-start(s32[4,8]{1,0:T(4,128)} %tissue.1) | copy-start | bytes 388

commit v2 on v1

--- a/solution.py
+++ b/solution.py
@@ -11,10 +11,12 @@
 LANES = 128
 MESH = pl.DeviceIdType.MESH
 LAG = 3
-
-
-def kernel(rows, cols, tissue, q_hbm, k_hbm, v_hbm, out_ref, kv, qv, bias, local_sem,
-           row_send, row_recv, col_send, col_recv):
+ROW_DEPTH = 2
+COL_DEPTH = 3
+
+
+def kernel(rows, cols, tissue_hbm, q_hbm, k_hbm, v_hbm, out_ref, kv, qv, bias, tissue, local_sem,
+           tissue_sem, row_send, row_recv, col_send, col_recv):
     chunks, _, _, tokens, _ = kv.shape
     r, c = lax.axis_index("row"), lax.axis_index("col")
     ring = rows == 4
@@ -33,10 +35,8 @@
             pltpu.make_async_copy(q_hbm.at[0, 0, :, lanes(i)], qv.at[i], local_sem.at[2, i]),
         ]
 
-    @pl.loop(0, chunks)
-    def _(i):
-        for copy in local_copies(i):
-            copy.start()
+    tissue_copy = pltpu.make_async_copy(tissue_hbm, tissue, tissue_sem)
+    tissue_copy.start()
 
     if ring:
         near = 1 - 2 * lax.rem(r, 2)
@@ -72,6 +72,12 @@
             barrier, inc=1, device_id=(r, other), device_id_type=MESH))
         count = count + cond.astype(jnp.int32)
 
+    @pl.loop(0, chunks)
+    def _(i):
+        for copy in local_copies(i):
+            copy.start()
+
+    tissue_copy.wait()
     for a in (-1, 0, 1):
         for b in (-1, 0, 1):
             s = slot(a, b)
@@ -108,27 +114,49 @@
             send_sem=col_send.at[direction, which, i], recv_sem=col_recv.at[direction, which, i],
             device_id=(r, c - b), device_id_type=MESH)
 
+    def row_starts(i):
+        for ch in (0, 1):
+            when(channels[ch][2], lambda: row_copy(ch, i).start())
+
     def col_sends(which, i):
         when(has_right, lambda: col_copy(0, which, i).start())
         when(has_left, lambda: col_copy(1, which, i).start())
 
+    depth = ROW_DEPTH if ring else chunks
+
     @pl.loop(0, chunks)
     def _(i):
         for copy in local_copies(i):
             copy.wait()
-        for ch in (0, 1):
-            if not (ring and ch == 1):
-                when(channels[ch][2], lambda: row_copy(ch, i).start())
-        col_sends(0, i)
+
+        @pl.when(i < depth)
+        def _():
+            if ring:
+                row_copy(0, i).start()
+            else:
+                row_starts(i)
+
+        pl.when(i < COL_DEPTH)(lambda: col_sends(0, i))
+
+    def first(i):
+        def step():
+            row_copy(0, i).wait_recv()
+            if ring:
+                when(channels[1][2], lambda: row_copy(1, i).start())
+                pl.when(i + depth < chunks)(lambda: row_copy(0, i + depth).start())
+            col_sends(1, i)
+        when(channels[0][0], step)
+        pl.when(i + COL_DEPTH < chunks)(lambda: col_sends(0, i + COL_DEPTH))
+
+    def second(i):
+        def step():
+            row_copy(1, i).wait_recv()
+            col_sends(2, i)
+        when(channels[1][0], step)
 
     def forward(i):
-        for ch in (0, 1):
-            def step():
-                row_copy(ch, i).wait_recv()
-                if ring and ch == 0:
-                    when(channels[1][2], lambda: row_copy(1, i).start())
-                col_sends(1 + ch, i)
-            when(channels[ch][0], step)
+        first(i)
+        pl.when(i > 0)(lambda: second(i - 1))
 
     own = tissue[r, c].astype(jnp.float32)
     low = lax.broadcasted_iota(jnp.int32, (tokens, LANES), 1) < HDIM
@@ -162,6 +190,8 @@
         forward(i)
         compute(i - LAG)
 
+    second(chunks - 1)
+
     @pl.loop(chunks - LAG, chunks)
     def _(i):
         compute(i)
@@ -181,24 +211,26 @@
 def on_device(rows, cols, query_states, key_states, value_states, tissue_map):
     _, _, tokens, features = query_states.shape
     chunks = features // LANES
-    any_space = pl.BlockSpec(memory_space=pl.ANY)
+    in_hbm = pl.BlockSpec(memory_space=pltpu.HBM)
     return pl.pallas_call(
         functools.partial(kernel, rows, cols),
         out_shape=jax.ShapeDtypeStruct(query_states.shape, jnp.bfloat16),
-        in_specs=[pl.BlockSpec(memory_space=pltpu.SMEM), any_space, any_space, any_space],
+        in_specs=[in_hbm] * 4,
         out_specs=pl.BlockSpec(memory_space=pltpu.VMEM),
         scratch_shapes=[
             pltpu.VMEM((chunks, 2, 9, tokens, LANES), jnp.bfloat16),
             pltpu.VMEM((chunks, tokens, LANES), jnp.bfloat16),
             pltpu.VMEM((8, 9 * tokens), jnp.float32),
+            pltpu.SMEM(tissue_map.shape, jnp.int32),
             pltpu.SemaphoreType.DMA((3, chunks)),
+            pltpu.SemaphoreType.DMA,
             pltpu.SemaphoreType.DMA((2, chunks)),
             pltpu.SemaphoreType.DMA((2, chunks)),
             pltpu.SemaphoreType.DMA((2, 3, chunks)),
             pltpu.SemaphoreType.DMA((2, 3, chunks)),
         ],
         compiler_params=pltpu.CompilerParams(
-            collective_id=0, has_side_effects=True, vmem_limit_bytes=40 * 1024 * 1024),
+            collective_id=0, has_side_effects=True, vmem_limit_bytes=63 * 1024 * 1024),
         cost_estimate=pl.CostEstimate(
             flops=4 * 9 * tokens * tokens * features, bytes_accessed=8 * tokens * features,
             transcendentals=9 * tokens * tokens * features // HDIM),

time: 27.4 us -> 25.5 us (0.931)
  local copies, waits for them, and re-layouts: 4.14 us -> 1.62 us
  Pallas kernels: 23 us -> 23.6 us
    unnamed x9 -> x1, local copies, waits for them, and re-layouts: 4.14 us -> 1.62 us
    pallas_call x1, Pallas kernels: 23 us -> 23.6 us  [on_device(): pl.pallas_call(functools.partial(kernel, rows, cols), out_shape=jax.Shape...]
where the time goes in v2:
time: 25.5 us; the launch traced here: 25.3 us
  Pallas kernels  23.6 us (93%)
  local copies, waits for them, and re-layouts  1.62 us (6%)
    pallas_call x1, Pallas kernels, on_device(): pl.pallas_call(functools.partial(kernel, rows, cols), out_shape=jax.Shape...  23.6 us
    unnamed x1, local copies, waits for them, and re-layouts  1.62 us

profile of v2, /device:TPU:3, one launch (start us, length us, event | category | flops | bytes accessed | tf_op | source)
XLA Modules:
  0.0 25.3 jit_solution(618323010612677907)
XLA Ops:
  0.0 23.6 %neighbourhood.1 = bf16[1,1,128,768]{3,2,1,0:T(8,128)(2,1)} custom-call(s32[4,8]{1,0:T(4,128)} %tissue_hbm.1, bf16[1,1,128,768]{3,2,1,0:T(8,128)(2,1)} %q_hbm.1, bf16[1,1,128,768]{3,2,1,0:T(8,128)(2,1)} %k_hbm.1, bf16[1,1,128,768]{3,2,1,0:T(8,128)(2,1)} %v_hbm.1), custom_call_target="tpu_custom_call" | custom-call | flops 452984832 | bytes 786432 | tf_op jit(solution)/shard_map/neighbourhood/pallas_call | solution.py:215
  23.7 1.6 %copy.6 = bf16[1,1,128,768]{3,2,1,0:T(8,128)(2,1)} copy(bf16[1,1,128,768]{3,2,1,0:T(8,128)(2,1)} %neighbourhood.1) | data formatting | bytes 393216

commit v3 on v2

--- a/solution.py
+++ b/solution.py
@@ -15,7 +15,7 @@
 COL_DEPTH = 3
 
 
-def kernel(rows, cols, tissue_hbm, q_hbm, k_hbm, v_hbm, out_ref, kv, qv, bias, tissue, local_sem,
+def kernel(rows, cols, tissue_hbm, q_hbm, k_hbm, v_hbm, out_ref, kv, raw, qt, tissue, local_sem,
            tissue_sem, row_send, row_recv, col_send, col_recv):
     chunks, _, _, tokens, _ = kv.shape
     r, c = lax.axis_index("row"), lax.axis_index("col")
@@ -31,8 +31,8 @@
     def local_copies(i):
         return [
             pltpu.make_async_copy(k_hbm.at[0, 0, :, lanes(i)], kv.at[i, 0, 4], local_sem.at[0, i]),
-            pltpu.make_async_copy(v_hbm.at[0, 0, :, lanes(i)], kv.at[i, 1, 4], local_sem.at[1, i]),
-            pltpu.make_async_copy(q_hbm.at[0, 0, :, lanes(i)], qv.at[i], local_sem.at[2, i]),
+            pltpu.make_async_copy(v_hbm.at[0, 0, :, lanes(i)], raw.at[1, i], local_sem.at[1, i]),
+            pltpu.make_async_copy(q_hbm.at[0, 0, :, lanes(i)], raw.at[0, i], local_sem.at[2, i]),
         ]
 
     tissue_copy = pltpu.make_async_copy(tissue_hbm, tissue, tissue_sem)
@@ -78,24 +78,36 @@
             copy.start()
 
     tissue_copy.wait()
+    shifts = []
     for a in (-1, 0, 1):
         for b in (-1, 0, 1):
             s = slot(a, b)
             if (a, b) == (0, 0):
-                bias[:, s * tokens:(s + 1) * tokens] = jnp.zeros((8, tokens), jnp.float32)
+                shifts.append(None)
                 continue
             inside = jnp.logical_and(jnp.logical_and(r + a >= 0, r + a < rows),
                                      jnp.logical_and(c + b >= 0, c + b < cols))
             entry = tissue[jnp.clip(r + a, 0, rows - 1), jnp.clip(c + b, 0, cols - 1)]
             live = jnp.where(inside, entry, 0) > 0
-            shift = jnp.where(live, jnp.float32(0), jnp.float32(-jnp.inf))
-            bias[:, s * tokens:(s + 1) * tokens] = jnp.full((8, tokens), shift, jnp.float32)
+            shifts.append(jnp.where(live, jnp.float32(0), jnp.float32(-jnp.inf)))
 
             @pl.when(jnp.logical_not(inside))
             def _():
                 @pl.loop(0, chunks)
                 def _(i):
                     kv[i, :, s] = jnp.zeros((2, tokens, LANES), kv.dtype)
+
+    low = lax.broadcasted_iota(jnp.int32, (LANES, tokens), 0) < HDIM
+
+    @pl.loop(0, chunks)
+    def _(i):
+        for copy in local_copies(i):
+            copy.wait()
+        kv[i, 1, 4] = raw[1, i].T
+        q = (raw[0, i] * jnp.bfloat16(HDIM ** -0.5)).T
+        zero = jnp.zeros_like(q)
+        qt[i, :, :tokens] = jnp.where(low, q, zero)
+        qt[i, :, tokens:] = jnp.where(low, zero, q)
 
     pl.semaphore_wait(barrier, count)
 
@@ -126,9 +138,6 @@
 
     @pl.loop(0, chunks)
     def _(i):
-        for copy in local_copies(i):
-            copy.wait()
-
         @pl.when(i < depth)
         def _():
             if ring:
@@ -159,7 +168,7 @@
         pl.when(i > 0)(lambda: second(i - 1))
 
     own = tissue[r, c].astype(jnp.float32)
-    low = lax.broadcasted_iota(jnp.int32, (tokens, LANES), 1) < HDIM
+    own = tissue[r, c].astype(jnp.float32)
 
     def compute(i):
         for direction, cond in ((0, has_left), (1, has_right)):
@@ -168,18 +177,20 @@
                 if which and channels[which - 1][0] is not None:
                     there = jnp.logical_and(cond, channels[which - 1][0])
                 when(there, lambda: col_copy(direction, which, i).wait_recv())
-        q = qv[i] * jnp.bfloat16(HDIM ** -0.5)
-        zero = jnp.zeros_like(q)
-        pair = jnp.concatenate([jnp.where(low, q, zero), jnp.where(low, zero, q)], axis=0)
-        keys = kv[i, 0].reshape(9 * tokens, LANES)
-        values = kv[i, 1].reshape(9 * tokens, LANES)
-        scores = lax.dot_general(pair, keys, (((1,), (1,)), ((), ())), preferred_element_type=jnp.float32)
-        scores = scores + bias[0:1, :]
-        weights = jnp.exp(scores - jnp.max(scores, axis=1, keepdims=True))
-        totals = jnp.sum(weights, axis=1, keepdims=True)
-        mixed = jnp.dot(weights.astype(jnp.bfloat16), values, preferred_element_type=jnp.float32)
+        queries = qt[i]
+        scores = []
+        for s, shift in enumerate(shifts):
+            tile = jnp.dot(kv[i, 0, s], queries, preferred_element_type=jnp.float32)
+            scores.append(tile if shift is None else tile + shift)
+        top = jnp.max(functools.reduce(jnp.maximum, scores), axis=0, keepdims=True)
+        weights = [jnp.exp(tile - top) for tile in scores]
+        totals = jnp.sum(functools.reduce(jnp.add, weights), axis=0, keepdims=True)
+        rounded = jnp.concatenate([tile.astype(jnp.bfloat16) for tile in weights], axis=0)
+        values = jnp.concatenate([kv[i, 1, s] for s in range(9)], axis=1)
+        mixed = jnp.dot(values, rounded, preferred_element_type=jnp.float32)
         mixed = mixed / totals * own
-        out_ref[0, 0, :, lanes(i)] = jnp.where(low, mixed[:tokens], mixed[tokens:]).astype(out_ref.dtype)
+        mixed = jnp.concatenate([mixed[:HDIM, :tokens], mixed[HDIM:, tokens:]], axis=0)
+        out_ref[0, 0, :, lanes(i)] = mixed.T.astype(out_ref.dtype)
 
     @pl.loop(0, LAG)
     def _(i):
@@ -214,13 +225,13 @@
     in_hbm = pl.BlockSpec(memory_space=pltpu.HBM)
     return pl.pallas_call(
         functools.partial(kernel, rows, cols),
-        out_shape=jax.ShapeDtypeStruct(query_states.shape, jnp.bfloat16),
+        out_shape=pltpu.VMEM(query_states.shape, jnp.bfloat16),
         in_specs=[in_hbm] * 4,
         out_specs=pl.BlockSpec(memory_space=pltpu.VMEM),
         scratch_shapes=[
             pltpu.VMEM((chunks, 2, 9, tokens, LANES), jnp.bfloat16),
-            pltpu.VMEM((chunks, tokens, LANES), jnp.bfloat16),
-            pltpu.VMEM((8, 9 * tokens), jnp.float32),
+            pltpu.VMEM((2, chunks, tokens, LANES), jnp.bfloat16),
+            pltpu.VMEM((chunks, LANES, 2 * tokens), jnp.bfloat16),
             pltpu.SMEM(tissue_map.shape, jnp.int32),
             pltpu.SemaphoreType.DMA((3, chunks)),
             pltpu.SemaphoreType.DMA,
@@ -230,7 +241,7 @@
             pltpu.SemaphoreType.DMA((2, 3, chunks)),
         ],
         compiler_params=pltpu.CompilerParams(
-            collective_id=0, has_side_effects=True, vmem_limit_bytes=63 * 1024 * 1024),
+            collective_id=0, has_side_effects=True, vmem_limit_bytes=60 * 1024 * 1024),
         cost_estimate=pl.CostEstimate(
             flops=4 * 9 * tokens * tokens * features, bytes_accessed=8 * tokens * features,
             transcendentals=9 * tokens * tokens * features // HDIM),

time: 25.5 us -> 24.1 us (0.945)
  local copies, waits for them, and re-layouts: 1.62 us -> 0.68 us
  Pallas kernels: 23.6 us -> 23.3 us
    unnamed x1, local copies, waits for them, and re-layouts: 1.62 us -> 0.68 us
    pallas_call x1, Pallas kernels: 23.6 us -> 23.3 us  [on_device(): pl.pallas_call(functools.partial(kernel, rows, cols), out_shape=pltpu.VME...]
where the time goes in v3:
time: 24.1 us; the launch traced here: 23.9 us
  Pallas kernels  23.3 us (97%)
  local copies, waits for them, and re-layouts  0.68 us (3%)
    pallas_call x1, Pallas kernels, on_device(): pl.pallas_call(functools.partial(kernel, rows, cols), out_shape=pltpu.VME...  23.3 us
    unnamed x1, local copies, waits for them, and re-layouts  0.68 us

profile of v3, /device:TPU:3, one launch (start us, length us, event | category | flops | bytes accessed | tf_op | source)
XLA Modules:
  0.0 23.9 jit_solution(4076651235140216218)
XLA Ops:
  0.0 23.3 %neighbourhood.1 = bf16[1,1,128,768]{3,2,1,0:T(8,128)(2,1)S(1)} custom-call(s32[4,8]{1,0:T(4,128)} %tissue_hbm.1, bf16[1,1,128,768]{3,2,1,0:T(8,128)(2,1)} %q_hbm.1, bf16[1,1,128,768]{3,2,1,0:T(8,128)(2,1)} %k_hbm.1, bf16[1,1,128,768]{3,2,1,0:T(8,128)(2,1)} %v_hbm.1), custom_call_target="tpu_custom_call" | custom-call | flops 452984832 | bytes 786432 | tf_op jit(solution)/shard_map/neighbourhood/pallas_call | solution.py:226
  23.3 0.7 %copy.6 = bf16[1,1,128,768]{3,2,1,0:T(8,128)(2,1)} copy(bf16[1,1,128,768]{3,2,1,0:T(8,128)(2,1)S(1)} %neighbourhood.1) | data formatting | bytes 393216

commit v4 on v3

--- a/solution.py
+++ b/solution.py
@@ -13,10 +13,12 @@
 LAG = 3
 ROW_DEPTH = 2
 COL_DEPTH = 3
+NEAR = (4, 6)
+FAR = (2, 4)
 
 
 def kernel(rows, cols, tissue_hbm, q_hbm, k_hbm, v_hbm, out_ref, kv, raw, qt, tissue, local_sem,
-           tissue_sem, row_send, row_recv, col_send, col_recv):
+           tissue_sem, row_send, row_recv, col_send, col_recv, cross_send, cross_recv):
     chunks, _, _, tokens, _ = kv.shape
     r, c = lax.axis_index("row"), lax.axis_index("col")
     ring = rows == 4
@@ -126,13 +128,35 @@
             send_sem=col_send.at[direction, which, i], recv_sem=col_recv.at[direction, which, i],
             device_id=(r, c - b), device_id_type=MESH)
 
+    odd = lax.rem(c, 2)
+    side = 2 * odd - 1
+    has_side = jnp.logical_and(c + side >= 0, c + side < cols)
+    spans = (NEAR, FAR) if ring else ((0, 0), (0, 0))
+
+    def moved(kind, i):
+        return jnp.logical_and(i >= spans[kind][0], i < spans[kind][1])
+
+    def cross_copy(kind, i):
+        source, target = (slot(0, side), r + near) if kind == 0 else (slot(near, side), across)
+        return pltpu.make_async_remote_copy(
+            src_ref=part(i, source), dst_ref=part(i, slot(-near, side)),
+            send_sem=cross_send.at[kind, i], recv_sem=cross_recv.at[kind, i],
+            device_id=(target, c), device_id_type=MESH)
+
+    def by_column(direction, which, i, sending):
+        if which == 0 or not ring:
+            return True
+        at_side = odd == (1 - direction if sending else direction)
+        return jnp.logical_not(jnp.logical_and(at_side, moved(which - 1, i)))
+
     def row_starts(i):
         for ch in (0, 1):
             when(channels[ch][2], lambda: row_copy(ch, i).start())
 
     def col_sends(which, i):
-        when(has_right, lambda: col_copy(0, which, i).start())
-        when(has_left, lambda: col_copy(1, which, i).start())
+        for direction, cond in ((0, has_right), (1, has_left)):
+            there = jnp.logical_and(cond, by_column(direction, which, i, True))
+            when(there, lambda: col_copy(direction, which, i).start())
 
     depth = ROW_DEPTH if ring else chunks
 
@@ -163,9 +187,20 @@
             col_sends(2, i)
         when(channels[1][0], step)
 
+    def cross(kind, i):
+        def step():
+            for d in (0, 1):
+                pl.when(odd == d)(lambda: col_copy(d, kind, i).wait_recv())
+            cross_copy(kind, i).start()
+        cond = has_side if kind == 0 else jnp.logical_and(has_side, outer)
+        pl.when(jnp.logical_and(cond, moved(kind, i)))(step)
+
     def forward(i):
         first(i)
         pl.when(i > 0)(lambda: second(i - 1))
+        if ring:
+            cross(0, i)
+            pl.when(i >= 2)(lambda: cross(1, i - 2))
 
     own = tissue[r, c].astype(jnp.float32)
     own = tissue[r, c].astype(jnp.float32)
@@ -176,7 +211,17 @@
                 there = cond
                 if which and channels[which - 1][0] is not None:
                     there = jnp.logical_and(cond, channels[which - 1][0])
+                there = jnp.logical_and(there, by_column(direction, which, i, False))
+                if ring and which < 2:
+                    passed = jnp.logical_and(odd == direction, moved(which, i))
+                    if which == 1:
+                        passed = jnp.logical_and(passed, outer)
+                    there = jnp.logical_and(there, jnp.logical_not(passed))
                 when(there, lambda: col_copy(direction, which, i).wait_recv())
+        if ring:
+            pl.when(jnp.logical_and(has_side, moved(0, i)))(lambda: cross_copy(0, i).wait_recv())
+            pl.when(jnp.logical_and(jnp.logical_and(has_side, inner), moved(1, i)))(
+                lambda: cross_copy(1, i).wait_recv())
         queries = qt[i]
         scores = []
         for s, shift in enumerate(shifts):
@@ -216,7 +261,12 @@
                 there = cond
                 if which and channels[which - 1][0] is not None:
                     there = jnp.logical_and(cond, channels[which - 1][0])
+                there = jnp.logical_and(there, by_column(direction, which, i, True))
                 when(there, lambda: col_copy(direction, which, i).wait_send())
+        if ring:
+            pl.when(jnp.logical_and(has_side, moved(0, i)))(lambda: cross_copy(0, i).wait_send())
+            pl.when(jnp.logical_and(jnp.logical_and(has_side, outer), moved(1, i)))(
+                lambda: cross_copy(1, i).wait_send())
 
 
 def on_device(rows, cols, query_states, key_states, value_states, tissue_map):
@@ -239,6 +289,8 @@
             pltpu.SemaphoreType.DMA((2, chunks)),
             pltpu.SemaphoreType.DMA((2, 3, chunks)),
             pltpu.SemaphoreType.DMA((2, 3, chunks)),
+            pltpu.SemaphoreType.DMA((2, chunks)),
+            pltpu.SemaphoreType.DMA((2, chunks)),
         ],
         compiler_params=pltpu.CompilerParams(
             collective_id=0, has_side_effects=True, vmem_limit_bytes=60 * 1024 * 1024),

time: 24.1 us -> 26.3 us (1.091)
  Pallas kernels: 23.3 us -> 25.5 us
    pallas_call x1, Pallas kernels: 23.3 us -> 25.5 us  [on_device(): pl.pallas_call(functools.partial(kernel, rows, cols), out_shape=pltpu.VME...]
where the time goes in v4:
time: 26.3 us; the launch traced here: 26.2 us
  Pallas kernels  25.5 us (97%)
  local copies, waits for them, and re-layouts  0.68 us (3%)
    pallas_call x1, Pallas kernels, on_device(): pl.pallas_call(functools.partial(kernel, rows, cols), out_shape=pltpu.VME...  25.5 us
    unnamed x1, local copies, waits for them, and re-layouts  0.68 us

profile of v4, /device:TPU:3, one launch (start us, length us, event | category | flops | bytes accessed | tf_op | source)
XLA Modules:
  0.0 26.2 jit_solution(86645808541313259)
XLA Ops:
  0.0 25.5 %neighbourhood.1 = bf16[1,1,128,768]{3,2,1,0:T(8,128)(2,1)S(1)} custom-call(s32[4,8]{1,0:T(4,128)} %tissue_hbm.1, bf16[1,1,128,768]{3,2,1,0:T(8,128)(2,1)} %q_hbm.1, bf16[1,1,128,768]{3,2,1,0:T(8,128)(2,1)} %k_hbm.1, bf16[1,1,128,768]{3,2,1,0:T(8,128)(2,1)} %v_hbm.1), custom_call_target="tpu_custom_call" | custom-call | flops 452984832 | bytes 786432 | tf_op jit(solution)/shard_map/neighbourhood/pallas_call | solution.py:276
  25.5 0.7 %copy.6 = bf16[1,1,128,768]{3,2,1,0:T(8,128)(2,1)} copy(bf16[1,1,128,768]{3,2,1,0:T(8,128)(2,1)S(1)} %neighbourhood.1) | data formatting | bytes 393216

commit v5 on v3

--- a/solution.py
+++ b/solution.py
@@ -10,9 +10,9 @@
 HDIM = 64
 LANES = 128
 MESH = pl.DeviceIdType.MESH
-LAG = 3
-ROW_DEPTH = 2
-COL_DEPTH = 3
+LAG = 4
+ROW_DEPTH = 3
+COL_DEPTH = 2
 
 
 def kernel(rows, cols, tissue_hbm, q_hbm, k_hbm, v_hbm, out_ref, kv, raw, qt, tissue, local_sem,

time: 24.1 us -> 24 us (level)
  no operation moved by 1% of the time
where the time goes in v5:
time: 24 us; the launch traced here: 23.8 us
  Pallas kernels  23.1 us (96%)
  local copies, waits for them, and re-layouts  0.68 us (3%)
    pallas_call x1, Pallas kernels, on_device(): pl.pallas_call(functools.partial(kernel, rows, cols), out_shape=pltpu.VME...  23.1 us
    unnamed x1, local copies, waits for them, and re-layouts  0.68 us

profile of v5, /device:TPU:3, one launch (start us, length us, event | category | flops | bytes accessed | tf_op | source)
XLA Modules:
  0.0 23.8 jit_solution(10750468060757305956)
XLA Ops:
  0.0 23.1 %neighbourhood.1 = bf16[1,1,128,768]{3,2,1,0:T(8,128)(2,1)S(1)} custom-call(s32[4,8]{1,0:T(4,128)} %tissue_hbm.1, bf16[1,1,128,768]{3,2,1,0:T(8,128)(2,1)} %q_hbm.1, bf16[1,1,128,768]{3,2,1,0:T(8,128)(2,1)} %k_hbm.1, bf16[1,1,128,768]{3,2,1,0:T(8,128)(2,1)} %v_hbm.1), custom_call_target="tpu_custom_call" | custom-call | flops 452984832 | bytes 786432 | tf_op jit(solution)/shard_map/neighbourhood/pallas_call | solution.py:226
  23.1 0.7 %copy.6 = bf16[1,1,128,768]{3,2,1,0:T(8,128)(2,1)} copy(bf16[1,1,128,768]{3,2,1,0:T(8,128)(2,1)S(1)} %neighbourhood.1) | data formatting | bytes 393216

commit v6 on v5

--- a/solution.py
+++ b/solution.py
@@ -21,6 +21,7 @@
     r, c = lax.axis_index("row"), lax.axis_index("col")
     ring = rows == 4
     has_up, has_down = r > 0, r < rows - 1
+    odd = lax.rem(c, 2) == 1
     has_left, has_right = c > 0, c < cols - 1
     slot = lambda a, b: (a + 1) * 3 + b + 1
     part = lambda i, s: kv.at[i, :, s]
@@ -131,8 +132,9 @@
             when(channels[ch][2], lambda: row_copy(ch, i).start())
 
     def col_sends(which, i):
-        when(has_right, lambda: col_copy(0, which, i).start())
+        pl.when(jnp.logical_and(has_right, odd))(lambda: col_copy(0, which, i).start())
         when(has_left, lambda: col_copy(1, which, i).start())
+        pl.when(jnp.logical_and(has_right, jnp.logical_not(odd)))(lambda: col_copy(0, which, i).start())
 
     depth = ROW_DEPTH if ring else chunks
 

time: 24 us -> 24 us (level)
  no operation moved by 1% of the time
where the time goes in v6:
time: 24 us; the launch traced here: 23.8 us
  Pallas kernels  23.1 us (96%)
  local copies, waits for them, and re-layouts  0.68 us (3%)
    pallas_call x1, Pallas kernels, on_device(): pl.pallas_call(functools.partial(kernel, rows, cols), out_shape=pltpu.VME...  23.1 us
    unnamed x1, local copies, waits for them, and re-layouts  0.68 us

profile of v6, /device:TPU:3, one launch (start us, length us, event | category | flops | bytes accessed | tf_op | source)
XLA Modules:
  0.0 23.8 jit_solution(15585618502215612759)
XLA Ops:
  0.0 23.1 %neighbourhood.1 = bf16[1,1,128,768]{3,2,1,0:T(8,128)(2,1)S(1)} custom-call(s32[4,8]{1,0:T(4,128)} %tissue_hbm.1, bf16[1,1,128,768]{3,2,1,0:T(8,128)(2,1)} %q_hbm.1, bf16[1,1,128,768]{3,2,1,0:T(8,128)(2,1)} %k_hbm.1, bf16[1,1,128,768]{3,2,1,0:T(8,128)(2,1)} %v_hbm.1), custom_call_target="tpu_custom_call" | custom-call | flops 452984832 | bytes 786432 | tf_op jit(solution)/shard_map/neighbourhood/pallas_call | solution.py:228
  23.1 0.7 %copy.6 = bf16[1,1,128,768]{3,2,1,0:T(8,128)(2,1)} copy(bf16[1,1,128,768]{3,2,1,0:T(8,128)(2,1)S(1)} %neighbourhood.1) | data formatting | bytes 393216

commit v7 on v5

--- a/solution.py
+++ b/solution.py
@@ -10,7 +10,7 @@
 HDIM = 64
 LANES = 128
 MESH = pl.DeviceIdType.MESH
-LAG = 4
+LAG = 3
 ROW_DEPTH = 3
 COL_DEPTH = 2
 
@@ -97,18 +97,6 @@
                 def _(i):
                     kv[i, :, s] = jnp.zeros((2, tokens, LANES), kv.dtype)
 
-    low = lax.broadcasted_iota(jnp.int32, (LANES, tokens), 0) < HDIM
-
-    @pl.loop(0, chunks)
-    def _(i):
-        for copy in local_copies(i):
-            copy.wait()
-        kv[i, 1, 4] = raw[1, i].T
-        q = (raw[0, i] * jnp.bfloat16(HDIM ** -0.5)).T
-        zero = jnp.zeros_like(q)
-        qt[i, :, :tokens] = jnp.where(low, q, zero)
-        qt[i, :, tokens:] = jnp.where(low, zero, q)
-
     pl.semaphore_wait(barrier, count)
 
     def row_copy(ch, i):
@@ -138,6 +126,10 @@
 
     @pl.loop(0, chunks)
     def _(i):
+        for copy in local_copies(i)[:2]:
+            copy.wait()
+        kv[i, 1, 4] = raw[1, i].T
+
         @pl.when(i < depth)
         def _():
             if ring:
@@ -146,6 +138,16 @@
                 row_starts(i)
 
         pl.when(i < COL_DEPTH)(lambda: col_sends(0, i))
+
+    low = lax.broadcasted_iota(jnp.int32, (LANES, tokens), 0) < HDIM
+
+    @pl.loop(0, chunks)
+    def _(i):
+        local_copies(i)[2].wait()
+        q = (raw[0, i] * jnp.bfloat16(HDIM ** -0.5)).T
+        zero = jnp.zeros_like(q)
+        qt[i, :, :tokens] = jnp.where(low, q, zero)
+        qt[i, :, tokens:] = jnp.where(low, zero, q)
 
     def first(i):
         def step():
@@ -199,11 +201,13 @@
     @pl.loop(LAG, chunks)
     def _(i):
         forward(i)
-        compute(i - LAG)
+        when(inner if ring else None, lambda: compute(i - LAG))
 
     second(chunks - 1)
 
-    @pl.loop(chunks - LAG, chunks)
+    begin = jnp.where(inner, chunks - LAG, 0) if ring else chunks - LAG
+
+    @pl.loop(begin, chunks)
     def _(i):
         compute(i)
 

time: 24 us -> 24.2 us (level)
  no operation moved by 1% of the time
where the time goes in v7:
time: 24.2 us; the launch traced here: 23.8 us
  Pallas kernels  23.1 us (95%)
  local copies, waits for them, and re-layouts  0.68 us (3%)
    pallas_call x1, Pallas kernels, on_device(): pl.pallas_call(functools.partial(kernel, rows, cols), out_shape=pltpu.VME...  23.1 us
    unnamed x1, local copies, waits for them, and re-layouts  0.68 us

profile of v7, /device:TPU:3, one launch (start us, length us, event | category | flops | bytes accessed | tf_op | source)
XLA Modules:
  0.0 23.8 jit_solution(16610040135043396142)
XLA Ops:
  0.0 23.1 %neighbourhood.1 = bf16[1,1,128,768]{3,2,1,0:T(8,128)(2,1)S(1)} custom-call(s32[4,8]{1,0:T(4,128)} %tissue_hbm.1, bf16[1,1,128,768]{3,2,1,0:T(8,128)(2,1)} %q_hbm.1, bf16[1,1,128,768]{3,2,1,0:T(8,128)(2,1)} %k_hbm.1, bf16[1,1,128,768]{3,2,1,0:T(8,128)(2,1)} %v_hbm.1), custom_call_target="tpu_custom_call" | custom-call | flops 452984832 | bytes 786432 | tf_op jit(solution)/shard_map/neighbourhood/pallas_call | solution.py:230
  23.2 0.7 %copy.6 = bf16[1,1,128,768]{3,2,1,0:T(8,128)(2,1)} copy(bf16[1,1,128,768]{3,2,1,0:T(8,128)(2,1)S(1)} %neighbourhood.1) | data formatting | bytes 393216

commit v8 on v7

--- a/solution.py
+++ b/solution.py
@@ -10,9 +10,9 @@
 HDIM = 64
 LANES = 128
 MESH = pl.DeviceIdType.MESH
-LAG = 3
+LAG = 4
 ROW_DEPTH = 3
-COL_DEPTH = 2
+COL_DEPTH = 6
 
 
 def kernel(rows, cols, tissue_hbm, q_hbm, k_hbm, v_hbm, out_ref, kv, raw, qt, tissue, local_sem,

time: 24.2 us -> 22.9 us (0.946)
  Pallas kernels: 23.1 us -> 21.8 us
    pallas_call x1, Pallas kernels: 23.1 us -> 21.8 us  [on_device(): pl.pallas_call(functools.partial(kernel, rows, cols), out_shape=pltpu.VME...]
where the time goes in v8:
time: 22.9 us; the launch traced here: 22.5 us
  Pallas kernels  21.8 us (95%)
  local copies, waits for them, and re-layouts  0.68 us (3%)
    pallas_call x1, Pallas kernels, on_device(): pl.pallas_call(functools.partial(kernel, rows, cols), out_shape=pltpu.VME...  21.8 us
    unnamed x1, local copies, waits for them, and re-layouts  0.68 us

profile of v8, /device:TPU:3, one launch (start us, length us, event | category | flops | bytes accessed | tf_op | source)
XLA Modules:
  0.0 22.5 jit_solution(1125501110812427911)
XLA Ops:
  0.0 21.8 %neighbourhood.1 = bf16[1,1,128,768]{3,2,1,0:T(8,128)(2,1)S(1)} custom-call(s32[4,8]{1,0:T(4,128)} %tissue_hbm.1, bf16[1,1,128,768]{3,2,1,0:T(8,128)(2,1)} %q_hbm.1, bf16[1,1,128,768]{3,2,1,0:T(8,128)(2,1)} %k_hbm.1, bf16[1,1,128,768]{3,2,1,0:T(8,128)(2,1)} %v_hbm.1), custom_call_target="tpu_custom_call" | custom-call | flops 452984832 | bytes 786432 | tf_op jit(solution)/shard_map/neighbourhood/pallas_call | solution.py:230
  21.9 0.7 %copy.6 = bf16[1,1,128,768]{3,2,1,0:T(8,128)(2,1)} copy(bf16[1,1,128,768]{3,2,1,0:T(8,128)(2,1)S(1)} %neighbourhood.1) | data formatting | bytes 393216

commit v9 on v8

--- a/solution.py
+++ b/solution.py
@@ -203,9 +203,11 @@
         forward(i)
         when(inner if ring else None, lambda: compute(i - LAG))
 
+    when(inner if ring else None, lambda: compute(chunks - LAG))
     second(chunks - 1)
 
-    begin = jnp.where(inner, chunks - LAG, 0) if ring else chunks - LAG
+    begin = chunks - LAG + 1
+    begin = jnp.where(inner, begin, 0) if ring else begin
 
     @pl.loop(begin, chunks)
     def _(i):

time: 22.9 us -> 23.4 us (1.022)
  Pallas kernels: 21.8 us -> 22.6 us
    pallas_call x1, Pallas kernels: 21.8 us -> 22.6 us  [on_device(): pl.pallas_call(functools.partial(kernel, rows, cols), out_shape=pltpu.VME...]
where the time goes in v9:
time: 23.4 us; the launch traced here: 23.2 us
  Pallas kernels  22.6 us (97%)
  local copies, waits for them, and re-layouts  0.68 us (3%)
    pallas_call x1, Pallas kernels, on_device(): pl.pallas_call(functools.partial(kernel, rows, cols), out_shape=pltpu.VME...  22.6 us
    unnamed x1, local copies, waits for them, and re-layouts  0.68 us

profile of v9, /device:TPU:3, one launch (start us, length us, event | category | flops | bytes accessed | tf_op | source)
XLA Modules:
  0.0 23.2 jit_solution(6676038448851392733)
XLA Ops:
  0.0 22.6 %neighbourhood.1 = bf16[1,1,128,768]{3,2,1,0:T(8,128)(2,1)S(1)} custom-call(s32[4,8]{1,0:T(4,128)} %tissue_hbm.1, bf16[1,1,128,768]{3,2,1,0:T(8,128)(2,1)} %q_hbm.1, bf16[1,1,128,768]{3,2,1,0:T(8,128)(2,1)} %k_hbm.1, bf16[1,1,128,768]{3,2,1,0:T(8,128)(2,1)} %v_hbm.1), custom_call_target="tpu_custom_call" | custom-call | flops 452984832 | bytes 786432 | tf_op jit(solution)/shard_map/neighbourhood/pallas_call | solution.py:232
  22.6 0.7 %copy.6 = bf16[1,1,128,768]{3,2,1,0:T(8,128)(2,1)} copy(bf16[1,1,128,768]{3,2,1,0:T(8,128)(2,1)S(1)} %neighbourhood.1) | data formatting | bytes 393216

commit v10 on v8

--- a/solution.py
+++ b/solution.py
@@ -10,7 +10,7 @@
 HDIM = 64
 LANES = 128
 MESH = pl.DeviceIdType.MESH
-LAG = 4
+LAG = 5
 ROW_DEPTH = 3
 COL_DEPTH = 6
 

time: 22.9 us -> 22.6 us (0.987)
  no operation moved by 1% of the time
where the time goes in v10:
time: 22.6 us; the launch traced here: 22.4 us
  Pallas kernels  21.7 us (96%)
  local copies, waits for them, and re-layouts  0.68 us (3%)
    pallas_call x1, Pallas kernels, on_device(): pl.pallas_call(functools.partial(kernel, rows, cols), out_shape=pltpu.VME...  21.7 us
    unnamed x1, local copies, waits for them, and re-layouts  0.68 us

profile of v10, /device:TPU:3, one launch (start us, length us, event | category | flops | bytes accessed | tf_op | source)
XLA Modules:
  0.0 22.4 jit_solution(9939655858179317800)
XLA Ops:
  0.0 21.7 %neighbourhood.1 = bf16[1,1,128,768]{3,2,1,0:T(8,128)(2,1)S(1)} custom-call(s32[4,8]{1,0:T(4,128)} %tissue_hbm.1, bf16[1,1,128,768]{3,2,1,0:T(8,128)(2,1)} %q_hbm.1, bf16[1,1,128,768]{3,2,1,0:T(8,128)(2,1)} %k_hbm.1, bf16[1,1,128,768]{3,2,1,0:T(8,128)(2,1)} %v_hbm.1), custom_call_target="tpu_custom_call" | custom-call | flops 452984832 | bytes 786432 | tf_op jit(solution)/shard_map/neighbourhood/pallas_call | solution.py:230
  21.8 0.7 %copy.6 = bf16[1,1,128,768]{3,2,1,0:T(8,128)(2,1)} copy(bf16[1,1,128,768]{3,2,1,0:T(8,128)(2,1)S(1)} %neighbourhood.1) | data formatting | bytes 393216

commit v11 on v8

--- a/solution.py
+++ b/solution.py
@@ -172,13 +172,15 @@
     own = tissue[r, c].astype(jnp.float32)
     own = tissue[r, c].astype(jnp.float32)
 
-    def compute(i):
+    def arrive(i):
         for direction, cond in ((0, has_left), (1, has_right)):
             for which in (0, 1, 2):
                 there = cond
                 if which and channels[which - 1][0] is not None:
                     there = jnp.logical_and(cond, channels[which - 1][0])
                 when(there, lambda: col_copy(direction, which, i).wait_recv())
+
+    def attend(i):
         queries = qt[i]
         scores = []
         for s, shift in enumerate(shifts):
@@ -194,6 +196,10 @@
         mixed = jnp.concatenate([mixed[:HDIM, :tokens], mixed[HDIM:, tokens:]], axis=0)
         out_ref[0, 0, :, lanes(i)] = mixed.T.astype(out_ref.dtype)
 
+    def compute(i):
+        arrive(i)
+        attend(i)
+
     @pl.loop(0, LAG)
     def _(i):
         forward(i)
@@ -205,11 +211,14 @@
 
     second(chunks - 1)
 
-    begin = jnp.where(inner, chunks - LAG, 0) if ring else chunks - LAG
-
-    @pl.loop(begin, chunks)
-    def _(i):
-        compute(i)
+    begin = jnp.where(inner, (chunks - LAG) // 2, 0) if ring else (chunks - LAG) // 2
+
+    @pl.loop(begin, chunks // 2)
+    def _(i):
+        arrive(2 * i)
+        arrive(2 * i + 1)
+        attend(2 * i)
+        attend(2 * i + 1)
 
     @pl.loop(0, chunks)
     def _(i):

time: 22.9 us -> 23.2 us (1.013)
  Pallas kernels: 21.8 us -> 22.2 us
    pallas_call x1, Pallas kernels: 21.8 us -> 22.2 us  [on_device(): pl.pallas_call(functools.partial(kernel, rows, cols), out_shape=pltpu.VME...]
where the time goes in v11:
time: 23.2 us; the launch traced here: 22.9 us
  Pallas kernels  22.2 us (96%)
  local copies, waits for them, and re-layouts  0.68 us (3%)
    pallas_call x1, Pallas kernels, on_device(): pl.pallas_call(functools.partial(kernel, rows, cols), out_shape=pltpu.VME...  22.2 us
    unnamed x1, local copies, waits for them, and re-layouts  0.68 us

profile of v11, /device:TPU:3, one launch (start us, length us, event | category | flops | bytes accessed | tf_op | source)
XLA Modules:
  0.0 22.9 jit_solution(15642166578650315000)
XLA Ops:
  0.0 22.2 %neighbourhood.1 = bf16[1,1,128,768]{3,2,1,0:T(8,128)(2,1)S(1)} custom-call(s32[4,8]{1,0:T(4,128)} %tissue_hbm.1, bf16[1,1,128,768]{3,2,1,0:T(8,128)(2,1)} %q_hbm.1, bf16[1,1,128,768]{3,2,1,0:T(8,128)(2,1)} %k_hbm.1, bf16[1,1,128,768]{3,2,1,0:T(8,128)(2,1)} %v_hbm.1), custom_call_target="tpu_custom_call" | custom-call | flops 452984832 | bytes 786432 | tf_op jit(solution)/shard_map/neighbourhood/pallas_call | solution.py:239
  22.2 0.7 %copy.6 = bf16[1,1,128,768]{3,2,1,0:T(8,128)(2,1)} copy(bf16[1,1,128,768]{3,2,1,0:T(8,128)(2,1)S(1)} %neighbourhood.1) | data formatting | bytes 393216

commit v12 on v10

--- a/solution.py
+++ b/solution.py
@@ -11,7 +11,7 @@
 LANES = 128
 MESH = pl.DeviceIdType.MESH
 LAG = 5
-ROW_DEPTH = 3
+ROW_DEPTH = 2
 COL_DEPTH = 6
 
 

time: 22.6 us -> 23.9 us (1.058)
  Pallas kernels: 21.7 us -> 23.1 us
    pallas_call x1, Pallas kernels: 21.7 us -> 23.1 us  [on_device(): pl.pallas_call(functools.partial(kernel, rows, cols), out_shape=pltpu.VME...]
where the time goes in v12:
time: 23.9 us; the launch traced here: 23.8 us
  Pallas kernels  23.1 us (97%)
  local copies, waits for them, and re-layouts  0.68 us (3%)
    pallas_call x1, Pallas kernels, on_device(): pl.pallas_call(functools.partial(kernel, rows, cols), out_shape=pltpu.VME...  23.1 us
    unnamed x1, local copies, waits for them, and re-layouts  0.68 us

profile of v12, /device:TPU:3, one launch (start us, length us, event | category | flops | bytes accessed | tf_op | source)
XLA Modules:
  0.0 23.8 jit_solution(5491202738414112021)
XLA Ops:
  0.0 23.1 %neighbourhood.1 = bf16[1,1,128,768]{3,2,1,0:T(8,128)(2,1)S(1)} custom-call(s32[4,8]{1,0:T(4,128)} %tissue_hbm.1, bf16[1,1,128,768]{3,2,1,0:T(8,128)(2,1)} %q_hbm.1, bf16[1,1,128,768]{3,2,1,0:T(8,128)(2,1)} %k_hbm.1, bf16[1,1,128,768]{3,2,1,0:T(8,128)(2,1)} %v_hbm.1), custom_call_target="tpu_custom_call" | custom-call | flops 452984832 | bytes 786432 | tf_op jit(solution)/shard_map/neighbourhood/pallas_call | solution.py:230
  23.1 0.7 %copy.6 = bf16[1,1,128,768]{3,2,1,0:T(8,128)(2,1)} copy(bf16[1,1,128,768]{3,2,1,0:T(8,128)(2,1)S(1)} %neighbourhood.1) | data formatting | bytes 393216
